TPU v7x, 512 devices: a whole 4x8x8 slice. The times are simulated.
512 devices in a mesh: band: 64 (over z, x, core), lev: 8 (over y).
Axes of the slice: x: 4, y: 8, z: 8, core: 2. Of those that a mesh axis runs over, the one named last changes fastest.
Arguments:
- control: bfloat16 [1280, 1280, 2, 128], P('band', 'lev'), may hold values from -6 to 6
- vertical_root: bfloat16 [1280, 128, 128], P('band'), may hold values from -0.5 to 0.5
- legendre: bfloat16 [1280, 32, 1280], P('band'), may hold values from -0.0034179688 to 0.0034179688
- wave_list: int32 [1280], replicated, may hold values from 0 to 1279, as said below
- row_length: int32 [32], replicated, may hold values from 2580 to 5136, as said below
Outputs:
- grid_field: float32 [64, 128, 5136], P('band', 'lev')
- grid_slope: float32 [64, 128, 5136], P('band', 'lev')
Inputs may be any that keep to these rules, and one draw needn't show every extreme that they name: `wave_list`: every zonal wavenumber from 0 to 1279 appears once. The first 10 slots of each owner hold 10 consecutive wavenumbers in increasing order, starting at a multiple of 10 below 640; its last 10 slots hold 1279 minus those, in the same order. `row_length`: each entry is 20 + 4 i for a latitude row index i from 640 to 1279, and both ends occur.
All inputs are finite; a program needn't handle non-finite values.
Results may differ from a plain program's by a relative error of at most 0.0057.
Values may be sent and summed in bfloat16 or wider, within the bound.
A program may use at most 128 MiB of HBM per device.

v0:
```python
import math

import jax
import jax.numpy as jnp
from jax import lax
from jax.sharding import PartitionSpec as P

M = 1280
LONMAX = 5136


def row_degree(rows, own_rows):
    half_rows = own_rows // 2
    block_pos = rows // own_rows
    within = rows % own_rows
    lower = block_pos * half_rows + within
    return jnp.where(within < half_rows, lower, M - 1 - (lower - half_rows))


def block_basis(wave_list, row_len):
    columns = jnp.arange(128, dtype=jnp.int32)
    phase_int = wave_list[:, None] * columns[None, :] % row_len
    angle_val = phase_int.astype(jnp.float32) * (2.0 * math.pi / row_len.astype(jnp.float32))
    weight_m = jnp.where(wave_list == 0, 1.0, 2.0).astype(jnp.float32)
    slope_m = weight_m * wave_list.astype(jnp.float32) / M
    cosine = jnp.cos(angle_val)
    sine_val = jnp.sin(angle_val)
    real_rows = jnp.concatenate([weight_m[:, None] * cosine, -slope_m[:, None] * sine_val], axis=1)
    imag_rows = jnp.concatenate([-weight_m[:, None] * sine_val, -slope_m[:, None] * cosine], axis=1)
    stacked = jnp.stack([real_rows, imag_rows], axis=1)
    return stacked.astype(jnp.bfloat16).reshape(2 * wave_list.shape[0], 256)


def twist_coeffs(coeffs, wave_list, row_len, starts):
    phase_int = wave_list[None, :] * starts[:, None] % row_len
    angle_val = phase_int.astype(jnp.float32) * (2.0 * math.pi / row_len.astype(jnp.float32))
    cosine = jnp.cos(angle_val)[:, :, None]
    sine_val = jnp.sin(angle_val)[:, :, None]
    real_part = coeffs[:, 0, :].astype(jnp.float32)[None]
    imag_part = coeffs[:, 1, :].astype(jnp.float32)[None]
    new_real = real_part * cosine - imag_part * sine_val
    new_imag = real_part * sine_val + imag_part * cosine
    twisted = jnp.stack([new_real, new_imag], axis=2).astype(jnp.bfloat16)
    return twisted.reshape(starts.shape[0], 2 * wave_list.shape[0], coeffs.shape[2])


def row_transform(coeffs, wave_list, row_len):
    block_count = (LONMAX + 127) // 128
    levels = coeffs.shape[2]
    basis_block = block_basis(wave_list, row_len)
    starts = 128 * jnp.arange(block_count, dtype=jnp.int32)
    twisted = twist_coeffs(coeffs, wave_list, row_len, starts)
    products = jnp.einsum("bkl,kt->lbt", twisted, basis_block, preferred_element_type=jnp.float32)
    field_row = products[:, :, :128].reshape(levels, block_count * 128)
    slope_row = products[:, :, 128:].reshape(levels, block_count * 128)
    inside = (jnp.arange(LONMAX, dtype=jnp.int32) < row_len)[None, :]
    zero_val = jnp.zeros((), jnp.float32)
    return (
        jnp.where(inside, field_row[:, :LONMAX], zero_val),
        jnp.where(inside, slope_row[:, :LONMAX], zero_val),
    )


def shards(control, vertical_root, legendre, wave_list, row_length):
    degrees_dev, group_size, complex_parts, levels = control.shape
    band_pos = lax.axis_index("band")
    level_pos = lax.axis_index("lev")
    degree = row_degree(
        band_pos * degrees_dev + jnp.arange(degrees_dev, dtype=jnp.int32), degrees_dev
    )
    group_waves = lax.dynamic_slice_in_dim(wave_list, level_pos * group_size, group_size)
    retained = degree[:, None] >= group_waves[None, :]
    masked = jnp.where(retained[:, :, None, None], control, jnp.zeros((), jnp.bfloat16))
    correlated = jnp.einsum(
        "nlk,nsck->nscl", vertical_root, masked, preferred_element_type=jnp.float32
    ).astype(jnp.bfloat16)
    by_level = lax.all_to_all(correlated, "lev", split_axis=3, concat_axis=1, tiled=True)
    spectral = lax.all_to_all(by_level, "band", split_axis=1, concat_axis=0, tiled=True)
    total_degrees, owned_count, complex_parts, level_share = spectral.shape
    owned_waves = lax.dynamic_slice_in_dim(wave_list, band_pos * owned_count, owned_count)
    all_degrees = row_degree(jnp.arange(total_degrees, dtype=jnp.int32), degrees_dev)
    parity = jnp.where((all_degrees[:, None] + owned_waves[None, :]) % 2 == 0, 1.0, -1.0).astype(
        jnp.bfloat16
    )
    spectral_rows = spectral.reshape(total_degrees, owned_count, complex_parts * level_share)
    flipped = spectral_rows * parity[:, :, None]
    northern = jnp.einsum(
        "khn,nkc->hkc", legendre, spectral_rows, preferred_element_type=jnp.float32
    )
    southern = jnp.einsum("khn,nkc->hkc", legendre, flipped, preferred_element_type=jnp.float32)
    fourier = jnp.concatenate([northern, southern[::-1]], axis=0).astype(jnp.bfloat16)
    lat_total = fourier.shape[0]
    north_rows = lat_total // 2
    fourier = fourier.reshape(lat_total, owned_count, complex_parts, level_share)
    lat_dev = lat_total // lax.axis_size("band")
    lat_pos = band_pos * lat_dev + 0
    mirror_pos = jnp.where(lat_pos < north_rows, lat_pos, lat_total - 1 - lat_pos)
    row_len = row_length[mirror_pos]
    field_row, slope_row = row_transform(
        lax.all_to_all(fourier, "band", split_axis=0, concat_axis=1, tiled=True)[0],
        wave_list,
        row_len,
    )
    fields = [field_row]
    slopes = [slope_row]
    grid_field = jnp.stack(fields)
    grid_slope = jnp.stack(slopes)
    return (grid_field, grid_slope)


def solution(mesh):
    placed = (P("band", "lev", None, None), P("band", None, None), P("band", None, None), P(), P())
    return jax.shard_map(
        shards,
        mesh=mesh,
        in_specs=placed,
        out_specs=(P("band", "lev", None), P("band", "lev", None)),
        check_vma=False,
    )
```

profile of v0, /device:TPU:1, one launch (start us, length us, event | category | flops | bytes accessed | tf_op | source)
XLA Modules:
  0.0 275.7 jit_solution(14902643408898826859)
XLA Ops:
  0.6 0.0 copy-start
  0.7 0.9 dynamic_slice.10
  1.6 0.1 broadcast_compare_fusion
  1.6 0.0 copy-start.9
  1.6 6.2 %broadcast_select_fusion = bf16[20,160,2,128]{3,2,1,0:T(2,128)(2,1)S(1)} fusion(bf16[20,160,2,128]{3,2,1,0:T(2,128)(2,1)} %param.5, pred[20,160]{1,0:T(8,128)(4,1)S(1)} %broadcast_compare_fusion), kind=kLoop, calls=%fused_computation.6 | loop fusion | flops 819200 | bytes 3280000 | tf_op jit(solution)/shard_map/jit(_where)/select_n | solution.py:73
  7.8 0.0 copy-done.9
  7.8 0.6 convolution_convert_fusion
  8.4 4.9 %copy.24 = bf16[20,160,2,128]{1,2,0,3:T(2,128)(2,1)} copy(bf16[20,160,2,128]{3,1,2,0:T(8,128)(2,1)S(1)} %convolution_convert_fusion) | data formatting | bytes 3276800 | tf_op jit(solution)/shard_map/convert_element_type | solution.py:76
  13.3 66.9 %all_to_all.42 = bf16[20,160,2,128]{1,2,0,3:T(2,128)(2,1)S(1)} all-to-all(bf16[20,160,2,128]{1,2,0,3:T(2,128)(2,1)} %copy.24), channel_id=1, replica_groups=mesh['band'=64,'lev'=8] {'lev'}, dimensions={3} | all-to-all | bytes 3276800 | tf_op jit(solution)/shard_map/all_to_all | solution.py:77
  80.2 2.2 copy.25
  82.4 12.4 %copy.34 = bf16[20,8,160,2,16]{0,4,3,2,1:T(8,128)(2,1)} copy(bf16[20,8,160,2,16]{2,4,1,3,0:T(8,128)(2,1)} %bitcast.73) | data formatting | bytes 3276800 | tf_op jit(solution)/shard_map/all_to_all | solution.py:77
  94.8 24.2 %reshape.250 = bf16[64,2,6400]{2,1,0:T(2,128)(2,1)} reshape(bf16[1280,2,16,20]{3,2,1,0:T(8,128)(2,1)} %bitcast.71) | data formatting | bytes 3276800
  119.0 0.0 copy-start.11
  119.0 0.0 copy-start.10
  119.0 17.6 %all-to-all-start.1 = ((bf16[64,2,6400]{2,1,0:T(2,128)(2,1)}), bf16[64,2,6400]{2,1,0:T(2,128)(2,1)S(1)}, u32[]{:S(2)}, u32[]{:S(2)}) async-start(bf16[64,2,6400]{2,1,0:T(2,128)(2,1)} %reshape.250), calls=%async_computation.1 | async-start | bytes 3276800 | tf_op jit(solution)/shard_map/all_to_all | solution.py:78
  136.7 0.0 copy-done.11
  136.7 0.6 dynamic_slice.9
  139.1 0.0 copy-done.10
  139.1 0.1 dynamic_slice.11
  139.3 0.1 select_convert_fusion
  139.5 4.2 %fusion.32 = (f32[41,1280]{1,0:T(8,128)}, f32[41,1280]{1,0:T(8,128)}) fusion(f32[]{:T(128)S(6)} %div.30, s32[]{:T(128)S(6)} %select_n.122, s32[41]{0:T(128)S(1)} %iota_multiply_fusion, s32[1280]{0:T(1024)S(1)} %copy-done.10, pred[]{:T(512)S(6)} %lt.80), kind=kLoop, calls=%fused_computation.48 | loop fusion | flops 524800 | bytes 425133 | tf_op jit(solution)/shard_map/cos | solution.py:37
  143.7 10.2 %multiply_convert_fusion.2 = (bf16[1280,128]{1,0:T(8,128)(2,1)}, bf16[1280,128]{1,0:T(8,128)(2,1)}, bf16[1280,128]{1,0:T(8,128)(2,1)}, bf16[1280,128]{1,0:T(8,128)(2,1)}) fusion(f32[1280]{0:T(1024)S(1)} %get-tuple-element.15, f32[]{:T(128)S(6)} %div.30, s32[]{:T(128)S(6)} %select_n.122, s32[1280]{0:T(1024)S(1)} %copy-done.10, pred[]{:T(512)S(6)} %lt.80, ...), kind=kLoop, calls=%fused_computation.26 | loop fusion | flops 2949120 | bytes 1331209 | tf_op jit(solution)/shard_map/convert.16
  153.9 23.0 %all-to-all-done.1 = bf16[64,2,6400]{2,1,0:T(2,128)(2,1)S(1)} async-done(((bf16[64,2,6400]{2,1,0:T(2,128)(2,1)}), bf16[64,2,6400]{2,1,0:T(2,128)(2,1)S(1)}, u32[]{:S(2)}, u32[]{:S(2)}) %all-to-all-start.1) | async-done | bytes 1638432 | tf_op jit(solution)/shard_map/all_to_all | solution.py:78
  176.9 27.9 %reshape.251 = bf16[1280,2,16,20]{3,2,1,0:T(8,128)(2,1)} reshape(bf16[64,2,6400]{2,1,0:T(2,128)(2,1)S(1)} %all-to-all-done.1) | data formatting | bytes 3276800
  204.8 20.2 %copy.29 = bf16[64,20,20,2,16]{1,0,4,3,2:T(8,128)(2,1)} copy(bf16[64,20,20,2,16]{1,4,3,2,0:T(8,128)(2,1)} %bitcast.72) | data formatting | bytes 3276800 | tf_op jit(solution)/shard_map/all_to_all | solution.py:78
  225.0 18.6 %reshape.242 = bf16[1280,20,32]{0,2,1:T(8,128)(2,1)S(1)} reshape(bf16[64,20,20,2,16]{1,0,4,3,2:T(8,128)(2,1)} %copy.29) | data formatting | bytes 3276800 | tf_op jit(solution)/shard_map/reshape | solution.py:85
  243.6 0.0 copy-done
  243.6 1.2 convolution_convert_fusion.1
  244.9 1.2 fusion.12
  246.1 0.0 copy-start.1
  246.1 0.0 copy-start.2
  246.1 0.0 copy-start.3
  246.1 0.0 copy-start.4
  246.1 1.1 rev.3
  247.3 1.7 pad_maximum_fusion
  249.0 1.8 copy.30
  250.8 1.3 reshape.252
  252.1 6.8 %all-to-all-start.2 = ((bf16[64,2,320]{2,1,0:T(2,128)(2,1)}), bf16[64,2,320]{2,1,0:T(2,128)(2,1)}, u32[]{:S(2)}, u32[]{:S(2)}) async-start(bf16[64,2,320]{2,1,0:T(2,128)(2,1)} %reshape.252), calls=%async_computation.2 | async-start | bytes 196608 | tf_op jit(solution)/shard_map/all_to_all | solution.py:100
  258.9 0.0 copy-done.1
  258.9 0.0 copy-done.2
  258.9 0.0 copy-done.3
  258.9 0.0 copy-done.4
  258.9 1.2 maximum_bitcast_fusion.4
  260.1 0.0 copy-start.5
  260.1 0.0 copy-start.6
  260.1 0.7 iota_compare_fusion
  260.8 8.6 %all-to-all-done.2 = bf16[64,2,320]{2,1,0:T(2,128)(2,1)} async-done(((bf16[64,2,320]{2,1,0:T(2,128)(2,1)}), bf16[64,2,320]{2,1,0:T(2,128)(2,1)}, u32[]{:S(2)}, u32[]{:S(2)}) %all-to-all-start.2) | async-done | bytes 81952 | tf_op jit(solution)/shard_map/all_to_all | solution.py:100
  269.4 1.6 reshape.253
  271.0 0.2 copy.31
  271.2 0.8 squeeze.9
  272.1 0.0 copy-done.5
  272.1 0.0 copy-done.6
  272.1 0.0 copy-start.7
  272.1 0.0 copy-start.8
  272.1 1.2 subtract_convert_fusion
  273.3 0.0 copy-done.7
  273.3 0.1 copy-done.8
  273.4 1.2 fusion.9
  274.6 0.1 fusion.51
  274.6 0.1 copy.44
  274.7 0.1 copy.45
  274.8 0.9 fusion.25
  (5 shorter events, 0.1 us)
Async XLA Ops:
  0.6 243.0 %copy-start = (bf16[20,32,1280]{2,1,0:T(8,128)(2,1)S(1)}, bf16[20,32,1280]{2,1,0:T(8,128)(2,1)}, u32[]{:S(2)}) copy-start(bf16[20,32,1280]{2,1,0:T(8,128)(2,1)} %param.7) | copy-start | bytes 4915204
  1.6 6.2 %copy-start.9 = (bf16[20,128,128]{2,1,0:T(8,128)(2,1)S(1)}, bf16[20,128,128]{2,1,0:T(8,128)(2,1)}, u32[]{:S(2)}) copy-start(bf16[20,128,128]{2,1,0:T(8,128)(2,1)} %param.6) | copy-start | bytes 1966084
  119.0 17.6 %copy-start.11 = (s32[32]{0:T(128)S(1)}, s32[32]{0:T(128)}, u32[]{:S(2)}) copy-start(s32[32]{0:T(128)} %param.9) | copy-start | bytes 388
  119.0 20.1 %copy-start.10 = (s32[1280]{0:T(1024)S(1)}, s32[1280]{0:T(1024)}, u32[]{:S(2)}) copy-start(s32[1280]{0:T(1024)} %param.8) | copy-start | bytes 15364
  119.0 57.9 %all-to-all-start.1 = ((bf16[64,2,6400]{2,1,0:T(2,128)(2,1)}), bf16[64,2,6400]{2,1,0:T(2,128)(2,1)S(1)}, u32[]{:S(2)}, u32[]{:S(2)}) async-start(bf16[64,2,6400]{2,1,0:T(2,128)(2,1)} %reshape.250), calls=%async_computation.1 | async-start | bytes 3276800 | tf_op jit(solution)/shard_map/all_to_all | solution.py:78
  246.1 12.8 %copy-start.1 = (bf16[1280,128]{1,0:T(8,128)(2,1)S(1)}, bf16[1280,128]{1,0:T(8,128)(2,1)}, u32[]{:S(2)}) copy-start(bf16[1280,128]{1,0:T(8,128)(2,1)} %get-tuple-element.8) | copy-start | bytes 983044
  246.1 12.8 %copy-start.2 = (bf16[1280,128]{1,0:T(8,128)(2,1)S(1)}, bf16[1280,128]{1,0:T(8,128)(2,1)}, u32[]{:S(2)}) copy-start(bf16[1280,128]{1,0:T(8,128)(2,1)} %get-tuple-element.9) | copy-start | bytes 983044
  246.1 12.8 %copy-start.3 = (bf16[1280,128]{1,0:T(8,128)(2,1)S(1)}, bf16[1280,128]{1,0:T(8,128)(2,1)}, u32[]{:S(2)}) copy-start(bf16[1280,128]{1,0:T(8,128)(2,1)} %get-tuple-element.12) | copy-start | bytes 983044
  246.1 12.8 %copy-start.4 = (bf16[1280,128]{1,0:T(8,128)(2,1)S(1)}, bf16[1280,128]{1,0:T(8,128)(2,1)}, u32[]{:S(2)}) copy-start(bf16[1280,128]{1,0:T(8,128)(2,1)} %get-tuple-element.16) | copy-start | bytes 983044
  252.1 17.3 %all-to-all-start.2 = ((bf16[64,2,320]{2,1,0:T(2,128)(2,1)}), bf16[64,2,320]{2,1,0:T(2,128)(2,1)}, u32[]{:S(2)}, u32[]{:S(2)}) async-start(bf16[64,2,320]{2,1,0:T(2,128)(2,1)} %reshape.252), calls=%async_computation.2 | async-start | bytes 196608 | tf_op jit(solution)/shard_map/all_to_all | solution.py:100
  260.1 11.9 %copy-start.5 = (f32[41,1280]{1,0:T(8,128)S(1)}, f32[41,1280]{1,0:T(8,128)}, u32[]{:S(2)}) copy-start(f32[41,1280]{1,0:T(8,128)} %get-tuple-element.10) | copy-start | bytes 629764
  260.1 11.9 %copy-start.6 = (f32[41,1280]{1,0:T(8,128)S(1)}, f32[41,1280]{1,0:T(8,128)}, u32[]{:S(2)}) copy-start(f32[41,1280]{1,0:T(8,128)} %get-tuple-element.11) | copy-start | bytes 629764
  272.1 1.2 copy-start.7
  272.1 1.3 copy-start.8
where the time goes:
time: 277 us; the launch traced here: 276 us
  local copies, waits for them, and re-layouts  119 us (43%)
  blocking collectives  66.9 us (24%)
  waiting for transfers between devices  31.6 us (11%)
  other arithmetic  26.5 us (10%)
  starting transfers between devices  24.4 us (9%)
  matrix products  4.23 us (2%)
  between operations  2.8 us (1%)
    all_to_all x1, blocking collectives, shards(): lax.all_to_all(correlated, 'lev', split_axis=3, concat_axis=1, tiled=True)  66.9 us
    unnamed x30, local copies, waits for them, and re-layouts  55.4 us
    all_to_all x1, waiting for transfers between devices, shards(): lax.all_to_all(by_level, 'band', split_axis=1, concat_axis=0, tiled=True)  23 us
    all_to_all x1, local copies, waits for them, and re-layouts, shards(): lax.all_to_all(by_level, 'band', split_axis=1, concat_axis=0, tiled=True)  20.2 us
    reshape x1, local copies, waits for them, and re-layouts, shards(): spectral.reshape(total_degrees, owned_count, complex_parts * level_share)  18.6 us
    all_to_all x1, starting transfers between devices, shards(): lax.all_to_all(by_level, 'band', split_axis=1, concat_axis=0, tiled=True)  17.6 us
    all_to_all x2, local copies, waits for them, and re-layouts, shards(): lax.all_to_all(correlated, 'lev', split_axis=3, concat_axis=1, tiled=True)  14.6 us
    another operation x2, other arithmetic  11.4 us
  transfers between devices with their start and end apart: 2, of which 2 were waited for; matrix products, arithmetic and copies ran while one was open for 6% of the time, Pallas kernels for 0%

commit v1 on v0

v1 whole, which is shorter than its diff:
```python
import functools

import jax
import jax.numpy as jnp
from jax import lax
from jax.experimental import pallas as pl
from jax.experimental.pallas import tpu as pltpu
from jax.sharding import PartitionSpec as P

M = 1280
LONMAX = 5136
BLOCKS = 41
F32 = jnp.float32
BF16 = jnp.bfloat16
MESH = pl.DeviceIdType.MESH

SIN_TERMS = (3.14159264, -5.16771008, 2.55007752, -0.598291286, 0.0776576603)
COS_TERMS = (0.999999953, -4.93479283, 4.05841135, -1.33187657, 0.219689611)


def iota(shape, dim):
    return lax.broadcasted_iota(jnp.int32, shape, dim)


def dot_nt(a, b):
    return lax.dot_general(a, b, (((1,), (1,)), ((), ())), preferred_element_type=F32)


def dot_nn(a, b):
    return lax.dot_general(a, b, (((1,), (0,)), ((), ())), preferred_element_type=F32)


def polynomial(terms, square):
    total = jnp.full_like(square, terms[-1])
    for term in terms[-2::-1]:
        total = total * square + term
    return total


def turn(product, row_len, inverse):
    doubled = product * 2.0
    halves = jnp.floor(doubled * inverse + 0.5)
    part = (doubled - halves * row_len) * inverse
    even = halves * 0.5
    sign = 1.0 - 4.0 * (even - jnp.floor(even))
    square = part * part
    return polynomial(COS_TERMS, square) * sign, polynomial(SIN_TERMS, square) * part * sign


def exchange(x):
    row, lane = iota((8, 128), 0), iota((8, 128), 1)
    for step in (4, 2, 1):
        row_bit = (row & step) != 0
        lane_bit = (lane & (16 * step)) != 0
        if step == 4:
            moved = pltpu.roll(pltpu.roll(x, 4, 0), 64, 1)
        else:
            up = pltpu.roll(pltpu.roll(x, step, 0), 128 - 16 * step, 1)
            down = pltpu.roll(pltpu.roll(x, 8 - step, 0), 16 * step, 1)
            moved = jnp.where(row_bit, up, down)
        x = jnp.where(row_bit == lane_bit, x, moved)
    return x


def kernel(
    ctrl_hbm, vert_hbm, leg_hbm, waves, rows_len,
    out_f, out_s,
    ctrl, vert, leg, prod, stage, send1, recv1, w0, w1, w2, w3, send2, recv2, cos_t, sin_t, basis, tw,
    in_sem, ssem1, rsem1, ssem2, rsem2,
):
    band, lev = lax.axis_index("band"), lax.axis_index("lev")
    z, rc = lax.div(band, 8), lax.rem(band, 8)
    xpos, core = lax.div(rc, 2), lax.rem(rc, 2)
    own_line = z == lev

    barrier = pltpu.get_barrier_semaphore()

    def greet(e, carry):
        @pl.when(jnp.logical_not(jnp.logical_and(e == band, own_line)))
        def _():
            pl.semaphore_signal(barrier, inc=1, device_id=(e, z), device_id_type=MESH)

        @pl.when(e != band)
        def _():
            pl.semaphore_signal(barrier, inc=1, device_id=(e, lev), device_id_type=MESH)

        return carry

    lax.fori_loop(0, 64, greet, 0)
    copies = [
        pltpu.make_async_copy(src, dst, in_sem.at[n])
        for n, (src, dst) in enumerate(((ctrl_hbm, ctrl), (vert_hbm, vert), (leg_hbm, leg)))
    ]
    for copy in copies:
        copy.start()
    stage[...] = jnp.zeros_like(stage)
    copies[0].wait()
    copies[1].wait()

    def products(q, carry):
        for h in range(2):
            n = q + 10 * h
            prod[n] = dot_nt(ctrl[n], vert[n])
        return carry

    lax.fori_loop(0, 10, products, 0)
    pl.semaphore_wait(barrier, jnp.where(own_line, 126, 127))

    row24 = iota((24, 128), 0)
    place24 = lax.shift_right_arithmetic(row24 - 4, 1)
    body24 = row24 >= 4

    def owner_step(d, carry):
        owner = lax.rem(xpos + lax.div(d, 2), 4) * 2 + lax.rem(core + d, 2)
        base = waves[(lev * 8 + owner) * 20]
        first = pl.multiple_of(owner * 40, 8)

        def degree_step(k, diag):
            high = prod[10 + k, pl.ds(first, 40), :]
            low = pltpu.roll(prod[k, pl.ds(first, 24), :], 4, 0)
            reach = 10 * band + k - base
            top = high[16:]
            mid = jnp.where(jnp.logical_and(body24, place24 <= reach), low, top)
            diag = jnp.where(jnp.logical_and(body24, place24 == reach), top, diag)
            parts = (high[:8], high[8:16], mid[:8], mid[8:16], mid[16:])
            places = (k, 16 + k, jnp.where(k < 6, 10 + k, 20 + k), 32 + k, 48 + k)
            for part, place in zip(parts, places):
                stage[pl.ds(place, 8, stride=64), :] = exchange(part)
            return diag

        diag = lax.fori_loop(0, 10, degree_step, jnp.zeros((24, 128), F32))
        for n, place in enumerate((30, 42, 58)):
            stage[pl.ds(place, 8, stride=64), :] = exchange(diag[8 * n : 8 * n + 8])
        for y in range(8):
            send1[d, y] = stage[64 * y : 64 * y + 64, :].astype(BF16)

        def send_step(e, inner):
            y = lax.rem(e + z + d, 8)
            mine = jnp.logical_and(jnp.logical_and(own_line, y == lev), owner == rc)

            @pl.when(jnp.logical_not(mine))
            def _():
                pltpu.make_async_remote_copy(
                    src_ref=send1.at[d, y], dst_ref=recv1.at[band], send_sem=ssem1, recv_sem=rsem1,
                    device_id=(lev * 8 + owner, y), device_id_type=MESH,
                ).start()

            @pl.when(mine)
            def _():
                pltpu.make_async_copy(send1.at[d, y], recv1.at[band], rsem1).start()

            return inner

        lax.fori_loop(0, 8, send_step, 0)
        return carry

    lax.fori_loop(0, 8, owner_step, 0)

    copies[2].wait()
    own_base = waves[band * 20]
    lane = iota((32, 128), 1)
    slot = lane & 15
    alt = (1 - 2 * (lane & 1)).astype(F32)
    diag_lane = slot == 10
    zero = jnp.zeros((32, 128), F32)
    late = slot >= 10
    late5 = jnp.logical_and(late, slot <= 14)

    def weigh(bb, carry):
        start = pl.multiple_of(lax.div(bb * 5, 4) * 128, 128)
        cols = pl.ds(pl.multiple_of(bb * 128, 128), 128)
        pick_row, pick_lane = iota((256, 128), 0), iota((256, 128), 1)
        pick_slot = pick_lane & 15
        target = 32 * lax.rem(bb, 4) + 20 * lax.shift_right_logical(pick_lane, 4) + pick_slot
        valid = pick_slot < 10
        pick_low = jnp.where(jnp.logical_and(valid, pick_row == target), 1.0, 0.0).astype(BF16)
        pick_high = jnp.where(jnp.logical_and(valid, pick_row == target + 10), 1.0, 0.0).astype(BF16)
        high = dot_nn(leg[:, pl.ds(start, 256)], pick_high)
        low = dot_nn(leg[:320, pl.ds(start, 256)], pick_low)
        degree = 10 * (8 * bb + lax.shift_right_logical(lane, 4)) + slot

        def put(group, place, parts):
            for n, part in enumerate(parts):
                at = pl.ds(place + 32 * n, 32)
                if group == 2:
                    w0[at, cols] = jnp.where(late, pltpu.roll(part, 10, 1), zero).astype(BF16)
                    w1[at, cols] = jnp.where(late5, pltpu.roll(part, 4, 1), zero).astype(BF16)
                else:
                    (w0, w1, None, w2, w3)[group][at, cols] = part.astype(BF16)

        for i in range(10):
            sign = 1.0 - 2.0 * (i % 2)
            part = high[32 * i : 32 * i + 32]
            place = (i % 4) * 64 if i < 8 else 256 + (i - 8) * 64
            put(i // 4, place, (part, part * (alt * -sign)))
        for i in range(10):
            sign = 1.0 - 2.0 * (i % 2)
            first = jnp.where(degree >= own_base + i, low[32 * i : 32 * i + 32], zero)
            part = high[320 + 32 * i : 352 + 32 * i]
            second = jnp.where(degree < own_base + i, part, zero)
            second = jnp.where(diag_lane, pltpu.roll(part, 10 - i, 1), second)
            signs = alt * sign
            place = 384 + i * 128 if i < 2 else ((i - 2) % 4) * 128
            put(
                (i + 2) // 4 + 2, place,
                (first, first * signs, second, second * jnp.where(diag_lane, 1.0, signs)),
            )
        return carry

    lax.fori_loop(0, 8, weigh, 0)

    row_len = rows_len[jnp.where(band < 32, band, 63 - band)].astype(F32)
    inverse = 1.0 / jnp.full((1, 128), row_len, F32)
    one_lane = iota((1, 128), 1)

    def gather_base(o, found):
        return jnp.where((one_lane & 63) == o, waves[o * 20], found)

    bases = lax.fori_loop(0, 64, gather_base, jnp.zeros((1, 128), jnp.int32))
    half = lax.shift_right_logical(one_lane, 6)

    def tables(tile, carry):
        fine = lax.rem(tile, 4)
        pair = lax.div(tile, 4)
        slots = jnp.where(pair == 2, 16 + 2 * fine + half, 8 * pair + 4 * half + fine)
        wave = jnp.where(slots < 10, bases + slots, M - 1 - bases - (slots - 10)).astype(F32)
        cols = pl.ds(pl.multiple_of(tile * 128, 128), 128)
        starts = iota((48, 128), 0).astype(F32) * 128.0
        cosine, sine = turn(starts * wave, row_len, inverse)
        cos_t[:, cols] = cosine
        sin_t[:, cols] = sine
        columns = iota((128, 128), 0).astype(F32)
        cosine, sine = turn(columns * wave, row_len, inverse)
        weight = jnp.where(wave == 0.0, 1.0, 2.0)
        slope = weight * wave * (1.0 / M)
        real = pl.ds(pl.multiple_of(tile * 128, 128), 128)
        imag = pl.ds(pl.multiple_of(1280 + tile * 128, 128), 128)
        basis[real, :128] = (cosine * weight).T.astype(BF16)
        basis[imag, :128] = (sine * -weight).T.astype(BF16)
        basis[real, 128:] = (sine * -slope).T.astype(BF16)
        basis[imag, 128:] = (cosine * -slope).T.astype(BF16)
        return carry

    lax.fori_loop(0, 10, tables, 0)

    pltpu.make_async_copy(recv1, recv1, rsem1).wait()
    wide = iota((64, 128), 1)
    chunk = lax.shift_right_logical(wide, 5)

    def rows16(n):
        return recv1[:, 16 * n : 16 * n + 16, :].reshape(1024, 128)

    def diagonal(value, start, step, where_chunks):
        total = None
        for n, at in enumerate(where_chunks):
            piece = value[start + step * n : start + step * n + 64]
            total = piece if total is None else jnp.where(chunk == at, piece, total)
        return total

    out0 = dot_nn(w0[...], rows16(0))
    out1 = dot_nn(w1[...], rows16(1))
    out2 = dot_nn(w2[...], rows16(2))
    out3 = dot_nn(w3[...], rows16(3))
    mixed = out0[256:] + out1[256:]
    every = (0, 1, 2, 3)
    lower = wide < 64
    back2 = pltpu.roll(diagonal(mixed, 128, 128, (2, 3)), 64, 1)
    back3 = pltpu.roll(diagonal(out2, 0, 128, every), 64, 1)
    back4 = pltpu.roll(diagonal(out3, 0, 128, every), 64, 1)
    groups = (
        diagonal(out0, 0, 64, every) + jnp.where(lower, back2, back3),
        diagonal(out1, 0, 64, every) + jnp.where(lower, back3, back4),
        jnp.where(lower, diagonal(mixed, 0, 64, (0, 1)) + back4, diagonal(mixed, 192, 128, (2, 3))),
        diagonal(out2, 64, 128, every),
        diagonal(out3, 64, 128, every),
    )
    for n, group in enumerate(groups):
        send2[pl.ds(n, 64, stride=8), :] = group

    def fourier_step(e, carry):
        lat = lax.rem(z + e, 8) * 8 + (rc ^ lax.div(e, 8))
        row = pl.multiple_of(jnp.where(lat < 32, lat, 95 - lat) * 8, 8)
        src, dst = send2.at[pl.ds(row, 8), :], recv2.at[pl.ds(pl.multiple_of(band * 8, 8), 8), :]

        @pl.when(lat != band)
        def _():
            pltpu.make_async_remote_copy(
                src_ref=src, dst_ref=dst, send_sem=ssem2, recv_sem=rsem2, device_id=(lat, lev), device_id_type=MESH
            ).start()

        @pl.when(lat == band)
        def _():
            pltpu.make_async_copy(src, dst, rsem2).start()

        return carry

    lax.fori_loop(0, 64, fourier_step, 0)
    pltpu.make_async_copy(recv2, recv2, rsem2).wait()

    def received(n):
        return recv2[pl.ds(n, 64, stride=8), :].astype(BF16).astype(F32)

    first_two = jnp.concatenate([received(0), received(1)], axis=0).T
    second_two = jnp.concatenate([received(2), received(3)], axis=0).T
    last_one = received(4)
    last_one = jnp.concatenate([last_one, last_one], axis=0).T
    left = iota((16, 128), 1) < 64

    def coefficients(part):
        tiles = []
        for source in (first_two, second_two):
            for fine in range(4):
                at = fine * 32 + part * 16
                tiles.append(source[at : at + 16])
        for fine in (0, 2):
            at = fine * 32 + part * 16
            tiles.append(jnp.where(left, last_one[at : at + 16], last_one[at + 32 : at + 48]))
        return tiles

    reals, imags = coefficients(0), coefficients(1)

    def twist(start, count):
        for tile in range(10):
            cols = slice(tile * 128, tile * 128 + 128)
            imag_cols = slice(1280 + tile * 128, 1408 + tile * 128)
            cosines, sines = cos_t[pl.ds(start, 8), cols], sin_t[pl.ds(start, 8), cols]
            real, imag = reals[tile], imags[tile]
            for n in range(count):
                at = pl.ds(pl.multiple_of((start + n) * 16, 16), 16)
                cosine, sine = cosines[n : n + 1], sines[n : n + 1]
                tw[at, cols] = (real * cosine - imag * sine).astype(BF16)
                tw[at, imag_cols] = (real * sine + imag * cosine).astype(BF16)

    def twist_step(n, carry):
        twist(pl.multiple_of(n * 8, 8), 8)
        return carry

    lax.fori_loop(0, 5, twist_step, 0)
    twist(40, 1)

    result = dot_nn(tw[...], basis[...])
    for b in range(BLOCKS):
        inside = (iota((16, 128), 1) + 128 * b).astype(F32) < row_len
        width = min(128, LONMAX - 128 * b)
        for out, at in ((out_f, 0), (out_s, 128)):
            piece = jnp.where(inside, result[16 * b : 16 * b + 16, at : at + 128], 0.0)
            out[0, :, 128 * b : 128 * b + width] = piece[:, :width]

    @pl.when(own_line)
    def _():
        pltpu.make_async_copy(send1_flat(send1), send1_flat(send1), ssem1).wait()

    @pl.when(jnp.logical_not(own_line))
    def _():
        pltpu.make_async_copy(send1, send1, ssem1).wait()

    pltpu.make_async_copy(send2.at[pl.ds(0, 504), :], send2.at[pl.ds(0, 504), :], ssem2).wait()


def send1_flat(send1):
    return send1.reshape(64, 64, 128).at[pl.ds(0, 63)]


def shards(control, vertical_root, legendre, wave_list, row_length):
    shape = jax.ShapeDtypeStruct((1, 16, LONMAX), F32)
    vmem, smem, hbm = (
        pl.BlockSpec(memory_space=pltpu.VMEM),
        pl.BlockSpec(memory_space=pltpu.SMEM),
        pl.BlockSpec(memory_space=pl.ANY),
    )
    return pl.pallas_call(
        kernel,
        out_shape=(shape, shape),
        in_specs=[hbm, hbm, hbm, smem, smem],
        out_specs=(vmem, vmem),
        scratch_shapes=[
            pltpu.VMEM((20, 320, 128), BF16),
            pltpu.VMEM((20, 128, 128), BF16),
            pltpu.VMEM((640, 1280), BF16),
            pltpu.VMEM((20, 320, 128), F32),
            pltpu.VMEM((512, 128), F32),
            pltpu.VMEM((8, 8, 64, 128), BF16),
            pltpu.VMEM((64, 64, 128), BF16),
            pltpu.VMEM((640, 1024), BF16),
            pltpu.VMEM((640, 1024), BF16),
            pltpu.VMEM((512, 1024), BF16),
            pltpu.VMEM((512, 1024), BF16),
            pltpu.VMEM((512, 128), F32),
            pltpu.VMEM((512, 128), F32),
            pltpu.VMEM((48, 1280), F32),
            pltpu.VMEM((48, 1280), F32),
            pltpu.VMEM((2560, 256), BF16),
            pltpu.VMEM((656, 2560), BF16),
            pltpu.SemaphoreType.DMA((3,)),
            pltpu.SemaphoreType.DMA,
            pltpu.SemaphoreType.DMA,
            pltpu.SemaphoreType.DMA,
            pltpu.SemaphoreType.DMA,
        ],
        compiler_params=pltpu.CompilerParams(
            collective_id=0, has_side_effects=True, vmem_limit_bytes=56 * 2**20
        ),
    )(
        control.reshape(20, 320, 128),
        vertical_root,
        legendre.reshape(640, 1280),
        wave_list,
        row_length,
    )


def solution(mesh):
    placed = (P("band", "lev", None, None), P("band", None, None), P("band", None, None), P(), P())
    return jax.shard_map(
        shards,
        mesh=mesh,
        in_specs=placed,
        out_specs=(P("band", "lev", None), P("band", "lev", None)),
        check_vma=False,
    )
```

time: 277 us -> 69.5 us (0.25)
  local copies, waits for them, and re-layouts: 119 us -> 3.45 us
  blocking collectives: 66.9 us -> 0 us
  Pallas kernels: 0 us -> 65.2 us
  waiting for transfers between devices: 31.6 us -> 0 us
  other arithmetic: 26.5 us -> 0 us
  starting transfers between devices: 24.4 us -> 0 us
  matrix products: 4.23 us -> 0 us
    all_to_all x1 -> x0, blocking collectives: 66.9 us -> none  [shards(): lax.all_to_all(correlated, 'lev', split_axis=3, concat_axis=1, tiled=True)]
    pallas_call x0 -> x1, Pallas kernels: none -> 65.2 us  [shards(): pl.pallas_call(kernel, out_shape=(shape, shape), in_specs=[hbm, hbm, hbm,...]
    unnamed x30 -> x2, local copies, waits for them, and re-layouts: 55.4 us -> 3.45 us
    all_to_all x4 -> x0, local copies, waits for them, and re-layouts: 35 us -> none  [the longest x1 20.2 us: shards(): lax.all_to_all(by_level, 'band', split_axis=1, concat_axis=0, tiled=True)]
    all_to_all x2 -> x0, waiting for transfers between devices: 31.6 us -> none  [the longest x1 23 us: shards(): lax.all_to_all(by_level, 'band', split_axis=1, concat_axis=0, tiled=True)]
    all_to_all x2 -> x0, starting transfers between devices: 24.4 us -> none  [the longest x1 17.6 us: shards(): lax.all_to_all(by_level, 'band', split_axis=1, concat_axis=0, tiled=True)]
    reshape x1 -> x0, local copies, waits for them, and re-layouts: 18.6 us -> none  [shards(): spectral.reshape(total_degrees, owned_count, complex_parts * level_share)]
    another operation x4 -> x0, other arithmetic: 13.5 us -> none
  transfers between devices with their start and end apart: 2 -> 0, of which waited for: 2 -> 0; matrix products, arithmetic and copies ran while one was open for 6% -> 0% of each run, Pallas kernels for 0% -> 0%
where the time goes in v1:
time: 69.5 us; the launch traced here: 69.3 us
  Pallas kernels  65.2 us (94%)
  local copies, waits for them, and re-layouts  3.45 us (5%)
    pallas_call x1, Pallas kernels, shards(): pl.pallas_call(kernel, out_shape=(shape, shape), in_specs=[hbm, hbm, hbm,...  65.2 us
    unnamed x2, local copies, waits for them, and re-layouts  3.45 us

profile of v1, /device:TPU:1, one launch (start us, length us, event | category | flops | bytes accessed | tf_op | source)
XLA Modules:
  0.0 69.3 jit_solution(11782157603416551970)
XLA Ops:
  0.6 65.2 %shard_map.68 = (f32[1,16,5136]{2,1,0:T(8,128)}, f32[1,16,5136]{2,1,0:T(8,128)}) custom-call(bf16[20,320,128]{2,1,0:T(8,128)(2,1)} %bitcast.2, bf16[20,128,128]{2,1,0:T(8,128)(2,1)} %vert_hbm.1, bf16[640,1280]{1,0:T(8,128)(2,1)} %bitcast.3, s32[1280]{0:T(1024)} %waves.1, s32[32]{0:T(128)} %rows_len.1), custom_call_target="tpu_custom_call" | custom-call | tf_op jit(solution)/shard_map/pallas_call | solution.py:371
  65.9 1.7 %copy.9 = f32[1,16,5136]{2,1,0:T(8,128)} copy(f32[1,16,5136]{2,1,0:T(8,128)} %get-tuple-element.4) | data formatting | bytes 657408
  67.6 1.7 %copy.10 = f32[1,16,5136]{2,1,0:T(8,128)} copy(f32[1,16,5136]{2,1,0:T(8,128)} %get-tuple-element.5) | data formatting | bytes 657408

commit v2 on v1

--- a/solution.py
+++ b/solution.py
@@ -47,25 +47,20 @@
     return polynomial(COS_TERMS, square) * sign, polynomial(SIN_TERMS, square) * part * sign
 
 
-def exchange(x):
-    row, lane = iota((8, 128), 0), iota((8, 128), 1)
-    for step in (4, 2, 1):
-        row_bit = (row & step) != 0
-        lane_bit = (lane & (16 * step)) != 0
-        if step == 4:
-            moved = pltpu.roll(pltpu.roll(x, 4, 0), 64, 1)
-        else:
-            up = pltpu.roll(pltpu.roll(x, step, 0), 128 - 16 * step, 1)
-            down = pltpu.roll(pltpu.roll(x, 8 - step, 0), 16 * step, 1)
-            moved = jnp.where(row_bit, up, down)
-        x = jnp.where(row_bit == lane_bit, x, moved)
-    return x
+def exchange(rows):
+    group = lax.shift_right_logical(iota((8, 128), 1), 4)
+    turned = [pltpu.roll(row, 16 * r, 1) if r else row for r, row in enumerate(rows)]
+    for step in (1, 2, 4):
+        odd = (group & step) != 0
+        turned = [jnp.where(odd, turned[(n + step) % 8], turned[n]) for n in range(8)]
+    found = [turned[(8 - y) % 8] for y in range(8)]
+    return [pltpu.roll(row, 128 - 16 * y, 1) if y else row for y, row in enumerate(found)]
 
 
 def kernel(
-    ctrl_hbm, vert_hbm, leg_hbm, waves, rows_len,
+    ctrl_hbm, vert_hbm, leg_hbm, waves_hbm, rows_hbm,
     out_f, out_s,
-    ctrl, vert, leg, prod, stage, send1, recv1, w0, w1, w2, w3, send2, recv2, cos_t, sin_t, basis, tw,
+    ctrl, vert, waves, leg, rows_len, prod, send1, recv1, w0, w1, w2, w3, send2, recv2, cos_t, sin_t, basis, tw,
     in_sem, ssem1, rsem1, ssem2, rsem2,
 ):
     band, lev = lax.axis_index("band"), lax.axis_index("lev")
@@ -73,6 +68,14 @@
     xpos, core = lax.div(rc, 2), lax.rem(rc, 2)
     own_line = z == lev
 
+    sources = (ctrl_hbm, vert_hbm, waves_hbm, leg_hbm, rows_hbm)
+    copies = [
+        pltpu.make_async_copy(src, dst, in_sem.at[n])
+        for n, (src, dst) in enumerate(zip(sources, (ctrl, vert, waves, leg, rows_len)))
+    ]
+    for copy in copies:
+        copy.start()
+
     barrier = pltpu.get_barrier_semaphore()
 
     def greet(e, carry):
@@ -87,52 +90,66 @@
         return carry
 
     lax.fori_loop(0, 64, greet, 0)
-    copies = [
-        pltpu.make_async_copy(src, dst, in_sem.at[n])
-        for n, (src, dst) in enumerate(((ctrl_hbm, ctrl), (vert_hbm, vert), (leg_hbm, leg)))
-    ]
-    for copy in copies:
-        copy.start()
-    stage[...] = jnp.zeros_like(stage)
     copies[0].wait()
     copies[1].wait()
 
     def products(q, carry):
-        for h in range(2):
-            n = q + 10 * h
-            prod[n] = dot_nt(ctrl[n], vert[n])
-        return carry
-
-    lax.fori_loop(0, 10, products, 0)
+        for n in range(5):
+            half = lax.div(q, 2)
+            degree = 5 * q + n
+            at = pl.multiple_of((degree + 6 * half) * 320, 8)
+            prod[pl.ds(at, 320), :] = dot_nt(ctrl[degree], vert[degree])
+        return carry
+
+    lax.fori_loop(0, 4, products, 0)
+    copies[2].wait()
     pl.semaphore_wait(barrier, jnp.where(own_line, 126, 127))
 
-    row24 = iota((24, 128), 0)
-    place24 = lax.shift_right_arithmetic(row24 - 4, 1)
-    body24 = row24 >= 4
+    sub = iota((8, 128), 0)
 
     def owner_step(d, carry):
         owner = lax.rem(xpos + lax.div(d, 2), 4) * 2 + lax.rem(core + d, 2)
         base = waves[(lev * 8 + owner) * 20]
-        first = pl.multiple_of(owner * 40, 8)
-
-        def degree_step(k, diag):
-            high = prod[10 + k, pl.ds(first, 40), :]
-            low = pltpu.roll(prod[k, pl.ds(first, 24), :], 4, 0)
-            reach = 10 * band + k - base
-            top = high[16:]
-            mid = jnp.where(jnp.logical_and(body24, place24 <= reach), low, top)
-            diag = jnp.where(jnp.logical_and(body24, place24 == reach), top, diag)
-            parts = (high[:8], high[8:16], mid[:8], mid[8:16], mid[16:])
-            places = (k, 16 + k, jnp.where(k < 6, 10 + k, 20 + k), 32 + k, 48 + k)
-            for part, place in zip(parts, places):
-                stage[pl.ds(place, 8, stride=64), :] = exchange(part)
-            return diag
-
-        diag = lax.fori_loop(0, 10, degree_step, jnp.zeros((24, 128), F32))
-        for n, place in enumerate((30, 42, 58)):
-            stage[pl.ds(place, 8, stride=64), :] = exchange(diag[8 * n : 8 * n + 8])
+        first = owner * 40
+        shift = 10 * band - base
+        on_diagonal = shift == 0
+
+        def load(half, k, row):
+            return prod[pl.ds(first + ((16 * half + k) * 320 + row), 8, stride=320), :]
+
+        def degrees(row, k):
+            high = load(1, k, row)
+            if row < 20:
+                return high
+            return jnp.where(sub + (k + shift) >= (row - 20) // 2, load(0, k, row - 20), high)
+
+        def diagonal_row(row, place):
+            if row < 20:
+                return jnp.zeros((8, 128), F32)
+            return jnp.where(on_diagonal, load(1, (row - 20) // 2 - place, row), 0.0)
+
+        def extra_a(r):
+            rows = jnp.where(sub < 6, diagonal_row(24 + r, 5), degrees(r, 2))
+            rows = jnp.where(sub < 5, degrees(24 + r, 5), rows)
+            rows = jnp.where(sub < 3, diagonal_row(32 + r, 2), rows)
+            return jnp.where(sub < 2, degrees(32 + r, 8), rows)
+
+        def extra_b(r):
+            rows = jnp.where(sub < 5, degrees(8 + r, 5), 0.0)
+            rows = jnp.where(sub < 3, diagonal_row(16 + r, 2), rows)
+            return jnp.where(sub < 2, degrees(16 + r, 8), rows)
+
+        def main(group):
+            return exchange([degrees(8 * group + r, 0) for r in range(8)])
+
+        for tile in range(3):
+            top = main(2 * tile)
+            low = main(2 * tile + 1) if tile < 2 else exchange([extra_a(r) for r in range(8)])
+            for y in range(8):
+                send1[8 * d + y, 16 * tile : 16 * tile + 16, :] = jnp.concatenate([top[y], low[y]], axis=0).astype(BF16)
+        low = exchange([extra_b(r) for r in range(8)])
         for y in range(8):
-            send1[d, y] = stage[64 * y : 64 * y + 64, :].astype(BF16)
+            send1[8 * d + y, 48:56, :] = low[y].astype(BF16)
 
         def send_step(e, inner):
             y = lax.rem(e + z + d, 8)
@@ -141,13 +158,13 @@
             @pl.when(jnp.logical_not(mine))
             def _():
                 pltpu.make_async_remote_copy(
-                    src_ref=send1.at[d, y], dst_ref=recv1.at[band], send_sem=ssem1, recv_sem=rsem1,
+                    src_ref=send1.at[8 * d + y], dst_ref=recv1.at[band], send_sem=ssem1, recv_sem=rsem1,
                     device_id=(lev * 8 + owner, y), device_id_type=MESH,
                 ).start()
 
             @pl.when(mine)
             def _():
-                pltpu.make_async_copy(send1.at[d, y], recv1.at[band], rsem1).start()
+                pltpu.make_async_copy(send1.at[8 * d + y], recv1.at[band], rsem1).start()
 
             return inner
 
@@ -156,15 +173,18 @@
 
     lax.fori_loop(0, 8, owner_step, 0)
 
-    copies[2].wait()
+    copies[3].wait()
+    copies[4].wait()
     own_base = waves[band * 20]
     lane = iota((32, 128), 1)
     slot = lane & 15
     alt = (1 - 2 * (lane & 1)).astype(F32)
     diag_lane = slot == 10
     zero = jnp.zeros((32, 128), F32)
-    late = slot >= 10
-    late5 = jnp.logical_and(late, slot <= 14)
+    early8 = slot < 8
+
+    def moved(part, by, low, high):
+        return jnp.where(jnp.logical_and(slot >= low, slot <= high), pltpu.roll(part, by % 128, 1), zero)
 
     def weigh(bb, carry):
         start = pl.multiple_of(lax.div(bb * 5, 4) * 128, 128)
@@ -181,17 +201,21 @@
 
         def put(group, place, parts):
             for n, part in enumerate(parts):
-                at = pl.ds(place + 32 * n, 32)
-                if group == 2:
-                    w0[at, cols] = jnp.where(late, pltpu.roll(part, 10, 1), zero).astype(BF16)
-                    w1[at, cols] = jnp.where(late5, pltpu.roll(part, 4, 1), zero).astype(BF16)
-                else:
-                    (w0, w1, None, w2, w3)[group][at, cols] = part.astype(BF16)
+                first8 = jnp.where(early8, part, zero)
+                targets = (
+                    ((w0, 0, first8), (w2, 1024, moved(part, 6, 14, 15))),
+                    ((w0, 256, moved(part, 8, 8, 15)), (w3, 384, moved(part, -5, 3, 4))),
+                    ((w1, 0, first8), (w3, 0, moved(part, -8, 0, 2))),
+                    ((w1, 384, moved(part, 8, 8, 15)), (w2, 512, moved(part, 3, 11, 13))),
+                    ((w2, 0, part),),
+                )[group]
+                for ref, start, value in targets:
+                    ref[pl.ds(start + place + 32 * n, 32), cols] = value.astype(BF16)
 
         for i in range(10):
             sign = 1.0 - 2.0 * (i % 2)
             part = high[32 * i : 32 * i + 32]
-            place = (i % 4) * 64 if i < 8 else 256 + (i - 8) * 64
+            place = (i % 4) * 64
             put(i // 4, place, (part, part * (alt * -sign)))
         for i in range(10):
             sign = 1.0 - 2.0 * (i % 2)
@@ -200,7 +224,7 @@
             second = jnp.where(degree < own_base + i, part, zero)
             second = jnp.where(diag_lane, pltpu.roll(part, 10 - i, 1), second)
             signs = alt * sign
-            place = 384 + i * 128 if i < 2 else ((i - 2) % 4) * 128
+            place = 128 + i * 128 if i < 2 else ((i - 2) % 4) * 128
             put(
                 (i + 2) // 4 + 2, place,
                 (first, first * signs, second, second * jnp.where(diag_lane, 1.0, signs)),
@@ -248,7 +272,10 @@
     chunk = lax.shift_right_logical(wide, 5)
 
     def rows16(n):
-        return recv1[:, 16 * n : 16 * n + 16, :].reshape(1024, 128)
+        if n < 3:
+            return recv1[:, 16 * n : 16 * n + 16, :].reshape(1024, 128)
+        rest = recv1[:, 48:56, :]
+        return jnp.concatenate([rest, jnp.zeros_like(rest)], axis=1).reshape(1024, 128)
 
     def diagonal(value, start, step, where_chunks):
         total = None
@@ -261,26 +288,30 @@
     out1 = dot_nn(w1[...], rows16(1))
     out2 = dot_nn(w2[...], rows16(2))
     out3 = dot_nn(w3[...], rows16(3))
-    mixed = out0[256:] + out1[256:]
+    sum0 = out0[:256] + out2[1024:]
+    sum1 = out0[256:] + out3[384:]
+    sum2 = out1[:384] + out3[:384]
+    sum3 = out1[384:] + out2[512:1024]
+    sum4 = out2[:512]
     every = (0, 1, 2, 3)
     lower = wide < 64
-    back2 = pltpu.roll(diagonal(mixed, 128, 128, (2, 3)), 64, 1)
-    back3 = pltpu.roll(diagonal(out2, 0, 128, every), 64, 1)
-    back4 = pltpu.roll(diagonal(out3, 0, 128, every), 64, 1)
+    back2 = pltpu.roll(diagonal(sum2, 128, 128, (2, 3)), 64, 1)
+    back3 = pltpu.roll(diagonal(sum3, 0, 128, every), 64, 1)
+    back4 = pltpu.roll(diagonal(sum4, 0, 128, every), 64, 1)
     groups = (
-        diagonal(out0, 0, 64, every) + jnp.where(lower, back2, back3),
-        diagonal(out1, 0, 64, every) + jnp.where(lower, back3, back4),
-        jnp.where(lower, diagonal(mixed, 0, 64, (0, 1)) + back4, diagonal(mixed, 192, 128, (2, 3))),
-        diagonal(out2, 64, 128, every),
-        diagonal(out3, 64, 128, every),
+        diagonal(sum0, 0, 64, every) + jnp.where(lower, back2, back3),
+        diagonal(sum1, 0, 64, every) + jnp.where(lower, back3, back4),
+        jnp.where(lower, diagonal(sum2, 0, 64, (0, 1)) + back4, diagonal(sum2, 192, 128, (2, 3))),
+        diagonal(sum3, 64, 128, every),
+        diagonal(sum4, 64, 128, every),
     )
     for n, group in enumerate(groups):
-        send2[pl.ds(n, 64, stride=8), :] = group
+        send2.reshape(512, 128)[pl.ds(n, 64, stride=8), :] = group
 
     def fourier_step(e, carry):
-        lat = lax.rem(z + e, 8) * 8 + (rc ^ lax.div(e, 8))
-        row = pl.multiple_of(jnp.where(lat < 32, lat, 95 - lat) * 8, 8)
-        src, dst = send2.at[pl.ds(row, 8), :], recv2.at[pl.ds(pl.multiple_of(band * 8, 8), 8), :]
+        lat = lax.rem(z + lax.div(e, 8), 8) * 8 + (rc ^ lax.rem(e, 8))
+        row = jnp.where(lat < 32, lat, 95 - lat)
+        src, dst = send2.at[row, pl.ds(0, 5), :], recv2.at[band, pl.ds(0, 5), :]
 
         @pl.when(lat != band)
         def _():
@@ -295,10 +326,11 @@
         return carry
 
     lax.fori_loop(0, 64, fourier_step, 0)
-    pltpu.make_async_copy(recv2, recv2, rsem2).wait()
+    arrived = recv2.at[:, pl.ds(0, 5), :]
+    pltpu.make_async_copy(arrived, arrived, rsem2).wait()
 
     def received(n):
-        return recv2[pl.ds(n, 64, stride=8), :].astype(BF16).astype(F32)
+        return recv2.reshape(512, 128)[pl.ds(n, 64, stride=8), :].astype(BF16).astype(F32)
 
     first_two = jnp.concatenate([received(0), received(1)], axis=0).T
     second_two = jnp.concatenate([received(2), received(3)], axis=0).T
@@ -348,50 +380,45 @@
 
     @pl.when(own_line)
     def _():
-        pltpu.make_async_copy(send1_flat(send1), send1_flat(send1), ssem1).wait()
+        sent = send1.at[pl.ds(0, 63)]
+        pltpu.make_async_copy(sent, sent, ssem1).wait()
 
     @pl.when(jnp.logical_not(own_line))
     def _():
         pltpu.make_async_copy(send1, send1, ssem1).wait()
 
-    pltpu.make_async_copy(send2.at[pl.ds(0, 504), :], send2.at[pl.ds(0, 504), :], ssem2).wait()
-
-
-def send1_flat(send1):
-    return send1.reshape(64, 64, 128).at[pl.ds(0, 63)]
+    gone = send2.at[pl.ds(0, 63), pl.ds(0, 5), :]
+    pltpu.make_async_copy(gone, gone, ssem2).wait()
 
 
 def shards(control, vertical_root, legendre, wave_list, row_length):
     shape = jax.ShapeDtypeStruct((1, 16, LONMAX), F32)
-    vmem, smem, hbm = (
-        pl.BlockSpec(memory_space=pltpu.VMEM),
-        pl.BlockSpec(memory_space=pltpu.SMEM),
-        pl.BlockSpec(memory_space=pl.ANY),
-    )
+    vmem, hbm = pl.BlockSpec(memory_space=pltpu.VMEM), pl.BlockSpec(memory_space=pl.ANY)
     return pl.pallas_call(
         kernel,
         out_shape=(shape, shape),
-        in_specs=[hbm, hbm, hbm, smem, smem],
+        in_specs=[hbm] * 5,
         out_specs=(vmem, vmem),
         scratch_shapes=[
             pltpu.VMEM((20, 320, 128), BF16),
             pltpu.VMEM((20, 128, 128), BF16),
+            pltpu.SMEM((1280,), jnp.int32),
             pltpu.VMEM((640, 1280), BF16),
-            pltpu.VMEM((20, 320, 128), F32),
-            pltpu.VMEM((512, 128), F32),
-            pltpu.VMEM((8, 8, 64, 128), BF16),
-            pltpu.VMEM((64, 64, 128), BF16),
+            pltpu.SMEM((32,), jnp.int32),
+            pltpu.VMEM((32 * 320, 128), F32),
+            pltpu.VMEM((64, 56, 128), BF16),
+            pltpu.VMEM((64, 56, 128), BF16),
+            pltpu.VMEM((512, 1024), BF16),
+            pltpu.VMEM((896, 1024), BF16),
+            pltpu.VMEM((1280, 1024), BF16),
             pltpu.VMEM((640, 1024), BF16),
-            pltpu.VMEM((640, 1024), BF16),
-            pltpu.VMEM((512, 1024), BF16),
-            pltpu.VMEM((512, 1024), BF16),
-            pltpu.VMEM((512, 128), F32),
-            pltpu.VMEM((512, 128), F32),
+            pltpu.VMEM((64, 8, 128), F32),
+            pltpu.VMEM((64, 8, 128), F32),
             pltpu.VMEM((48, 1280), F32),
             pltpu.VMEM((48, 1280), F32),
             pltpu.VMEM((2560, 256), BF16),
             pltpu.VMEM((656, 2560), BF16),
-            pltpu.SemaphoreType.DMA((3,)),
+            pltpu.SemaphoreType.DMA((5,)),
             pltpu.SemaphoreType.DMA,
             pltpu.SemaphoreType.DMA,
             pltpu.SemaphoreType.DMA,

time: 69.5 us -> 63.3 us (0.911)
  Pallas kernels: 65.2 us -> 59 us
    pallas_call x1, Pallas kernels: 65.2 us -> 59 us  [shards(): pl.pallas_call(kernel, out_shape=(shape, shape), in_specs=[hbm] * 5, out_...]
where the time goes in v2:
time: 63.3 us; the launch traced here: 63.1 us
  Pallas kernels  59 us (93%)
  local copies, waits for them, and re-layouts  3.45 us (5%)
  between operations  0.64 us (1%)
    pallas_call x1, Pallas kernels, shards(): pl.pallas_call(kernel, out_shape=(shape, shape), in_specs=[hbm] * 5, out_...  59 us
    unnamed x2, local copies, waits for them, and re-layouts  3.45 us

profile of v2, /device:TPU:1, one launch (start us, length us, event | category | flops | bytes accessed | tf_op | source)
XLA Modules:
  0.0 63.1 jit_solution(10573414239034775718)
XLA Ops:
  0.6 59.0 %shard_map.68 = (f32[1,16,5136]{2,1,0:T(8,128)}, f32[1,16,5136]{2,1,0:T(8,128)}) custom-call(bf16[20,320,128]{2,1,0:T(8,128)(2,1)} %bitcast.2, bf16[20,128,128]{2,1,0:T(8,128)(2,1)} %vert_hbm.1, bf16[640,1280]{1,0:T(8,128)(2,1)} %bitcast.3, s32[1280]{0:T(1024)} %waves_hbm.1, s32[32]{0:T(128)} %rows_hbm.1), custom_call_target="tpu_custom_call" | custom-call | tf_op jit(solution)/shard_map/pallas_call | solution.py:397
  59.7 1.7 %copy.9 = f32[1,16,5136]{2,1,0:T(8,128)} copy(f32[1,16,5136]{2,1,0:T(8,128)} %get-tuple-element.4) | data formatting | bytes 657408
  61.4 1.7 %copy.10 = f32[1,16,5136]{2,1,0:T(8,128)} copy(f32[1,16,5136]{2,1,0:T(8,128)} %get-tuple-element.5) | data formatting | bytes 657408

commit v3 on v2

--- a/solution.py
+++ b/solution.py
@@ -59,20 +59,30 @@
 
 def kernel(
     ctrl_hbm, vert_hbm, leg_hbm, waves_hbm, rows_hbm,
-    out_f, out_s,
+    blocks,
     ctrl, vert, waves, leg, rows_len, prod, send1, recv1, w0, w1, w2, w3, send2, recv2, cos_t, sin_t, basis, tw,
-    in_sem, ssem1, rsem1, ssem2, rsem2,
+    acc0, acc1, acc2, acc3,
+    in_sem, ctrl_sem, vert_sem, ssem1, rsem1, ssem2, rsem2, told1, told2,
 ):
     band, lev = lax.axis_index("band"), lax.axis_index("lev")
     z, rc = lax.div(band, 8), lax.rem(band, 8)
     xpos, core = lax.div(rc, 2), lax.rem(rc, 2)
     own_line = z == lev
 
-    sources = (ctrl_hbm, vert_hbm, waves_hbm, leg_hbm, rows_hbm)
+    def chunk_copies(q):
+        rows = pl.ds(5 * q, 5)
+        return (
+            pltpu.make_async_copy(ctrl_hbm.at[rows], ctrl.at[rows], ctrl_sem.at[q]),
+            pltpu.make_async_copy(vert_hbm.at[rows], vert.at[rows], vert_sem.at[q]),
+        )
+
     copies = [
         pltpu.make_async_copy(src, dst, in_sem.at[n])
-        for n, (src, dst) in enumerate(zip(sources, (ctrl, vert, waves, leg, rows_len)))
+        for n, (src, dst) in enumerate(((waves_hbm, waves), (leg_hbm, leg), (rows_hbm, rows_len)))
     ]
+    for q in range(4):
+        for copy in chunk_copies(q):
+            copy.start()
     for copy in copies:
         copy.start()
 
@@ -83,17 +93,12 @@
         def _():
             pl.semaphore_signal(barrier, inc=1, device_id=(e, z), device_id_type=MESH)
 
-        @pl.when(e != band)
-        def _():
-            pl.semaphore_signal(barrier, inc=1, device_id=(e, lev), device_id_type=MESH)
-
         return carry
 
     lax.fori_loop(0, 64, greet, 0)
-    copies[0].wait()
-    copies[1].wait()
-
     def products(q, carry):
+        for copy in chunk_copies(q):
+            copy.wait()
         for n in range(5):
             half = lax.div(q, 2)
             degree = 5 * q + n
@@ -102,8 +107,21 @@
         return carry
 
     lax.fori_loop(0, 4, products, 0)
-    copies[2].wait()
-    pl.semaphore_wait(barrier, jnp.where(own_line, 126, 127))
+    copies[0].wait()
+    pl.semaphore_wait(barrier, jnp.where(own_line, 63, 64))
+
+    def tell(sem, targets):
+        for n, target in enumerate(targets):
+
+            def signal(target=target):
+                pl.semaphore_signal(sem, inc=1, device_id=target, device_id_type=MESH)
+
+            if n:
+                signal()
+            else:
+                pl.when(jnp.logical_not(own_line))(signal)
+
+    tell(told1, [(lev * 8 + rc, lax.rem(lev + n, 8)) for n in range(8)])
 
     sub = iota((8, 128), 0)
 
@@ -151,30 +169,31 @@
         for y in range(8):
             send1[8 * d + y, 48:56, :] = low[y].astype(BF16)
 
-        def send_step(e, inner):
-            y = lax.rem(e + z + d, 8)
-            mine = jnp.logical_and(jnp.logical_and(own_line, y == lev), owner == rc)
-
-            @pl.when(jnp.logical_not(mine))
-            def _():
+        for e in (4, 3, 5, 2, 6, 1, 7, 0):
+            y = lax.rem(lev + e, 8)
+
+            def send(y=y, e=e):
                 pltpu.make_async_remote_copy(
-                    src_ref=send1.at[8 * d + y], dst_ref=recv1.at[band], send_sem=ssem1, recv_sem=rsem1,
+                    src_ref=send1.at[8 * d + y], dst_ref=recv1.at[band], send_sem=ssem1, recv_sem=rsem1.at[z],
                     device_id=(lev * 8 + owner, y), device_id_type=MESH,
                 ).start()
 
+            if e > 0:
+                send()
+                continue
+            mine = jnp.logical_and(own_line, d == 0)
+            pl.when(jnp.logical_not(mine))(send)
+
             @pl.when(mine)
-            def _():
-                pltpu.make_async_copy(send1.at[8 * d + y], recv1.at[band], rsem1).start()
-
-            return inner
-
-        lax.fori_loop(0, 8, send_step, 0)
+            def _(y=y):
+                pltpu.make_async_copy(send1.at[8 * d + y], recv1.at[band], rsem1.at[z]).start()
+
         return carry
 
     lax.fori_loop(0, 8, owner_step, 0)
 
-    copies[3].wait()
-    copies[4].wait()
+    copies[1].wait()
+    copies[2].wait()
     own_base = waves[band * 20]
     lane = iota((32, 128), 1)
     slot = lane & 15
@@ -232,6 +251,8 @@
         return carry
 
     lax.fori_loop(0, 8, weigh, 0)
+    pl.semaphore_wait(told1, jnp.where(own_line, 7, 8))
+    tell(told2, [(lev * 8 + (rc ^ n), z) for n in range(8)])
 
     row_len = rows_len[jnp.where(band < 32, band, 63 - band)].astype(F32)
     inverse = 1.0 / jnp.full((1, 128), row_len, F32)
@@ -267,15 +288,15 @@
 
     lax.fori_loop(0, 10, tables, 0)
 
-    pltpu.make_async_copy(recv1, recv1, rsem1).wait()
     wide = iota((64, 128), 1)
     chunk = lax.shift_right_logical(wide, 5)
 
-    def rows16(n):
+    def rows16(n, first, last):
+        count = 16 * (last - first)
         if n < 3:
-            return recv1[:, 16 * n : 16 * n + 16, :].reshape(1024, 128)
-        rest = recv1[:, 48:56, :]
-        return jnp.concatenate([rest, jnp.zeros_like(rest)], axis=1).reshape(1024, 128)
+            return recv1[first:last, 16 * n : 16 * n + 16, :].reshape(count, 128)
+        rest = recv1[first:last, 48:56, :]
+        return jnp.concatenate([rest, jnp.zeros_like(rest)], axis=1).reshape(count, 128)
 
     def diagonal(value, start, step, where_chunks):
         total = None
@@ -284,10 +305,15 @@
             total = piece if total is None else jnp.where(chunk == at, piece, total)
         return total
 
-    out0 = dot_nn(w0[...], rows16(0))
-    out1 = dot_nn(w1[...], rows16(1))
-    out2 = dot_nn(w2[...], rows16(2))
-    out3 = dot_nn(w3[...], rows16(3))
+    outs = None
+    for first, last in ((0, 4), (4, 6), (6, 8)):
+        for group in range(first, last):
+            part = recv1.at[pl.ds(8 * group, 8)]
+            pltpu.make_async_copy(part, part, rsem1.at[group]).wait()
+        for n, acc in enumerate((acc0, acc1, acc2, acc3)):
+            sums = dot_nn((w0, w1, w2, w3)[n][:, 128 * first : 128 * last], rows16(n, 8 * first, 8 * last))
+            acc[...] = acc[...] + sums if first else sums
+    out0, out1, out2, out3 = acc0[...], acc1[...], acc2[...], acc3[...]
     sum0 = out0[:256] + out2[1024:]
     sum1 = out0[256:] + out3[384:]
     sum2 = out1[:384] + out3[:384]
@@ -308,24 +334,23 @@
     for n, group in enumerate(groups):
         send2.reshape(512, 128)[pl.ds(n, 64, stride=8), :] = group
 
+    def fourier_row(lat):
+        row = jnp.where(lat < 32, lat, 95 - lat)
+        return send2.at[row, pl.ds(0, 5), :], recv2.at[band, pl.ds(0, 5), :]
+
     def fourier_step(e, carry):
-        lat = lax.rem(z + lax.div(e, 8), 8) * 8 + (rc ^ lax.rem(e, 8))
-        row = jnp.where(lat < 32, lat, 95 - lat)
-        src, dst = send2.at[row, pl.ds(0, 5), :], recv2.at[band, pl.ds(0, 5), :]
-
-        @pl.when(lat != band)
-        def _():
-            pltpu.make_async_remote_copy(
-                src_ref=src, dst_ref=dst, send_sem=ssem2, recv_sem=rsem2, device_id=(lat, lev), device_id_type=MESH
-            ).start()
-
-        @pl.when(lat == band)
-        def _():
-            pltpu.make_async_copy(src, dst, rsem2).start()
-
-        return carry
-
-    lax.fori_loop(0, 64, fourier_step, 0)
+        lat = lax.rem(z + 4 + 3 * lax.div(e, 8), 8) * 8 + (rc ^ lax.rem(e, 8))
+        src, dst = fourier_row(lat)
+        pltpu.make_async_remote_copy(
+            src_ref=src, dst_ref=dst, send_sem=ssem2, recv_sem=rsem2, device_id=(lat, lev), device_id_type=MESH
+        ).start()
+        return carry
+
+    pl.semaphore_wait(told2, jnp.where(own_line, 7, 8))
+    src, dst = fourier_row(band)
+    pltpu.make_async_copy(src, dst, rsem2).start()
+    lax.fori_loop(0, 32, fourier_step, 0)
+    lax.fori_loop(33, 64, fourier_step, 0)
     arrived = recv2.at[:, pl.ds(0, 5), :]
     pltpu.make_async_copy(arrived, arrived, rsem2).wait()
 
@@ -371,12 +396,10 @@
     twist(40, 1)
 
     result = dot_nn(tw[...], basis[...])
+    column = iota((16, 256), 1) & 127
     for b in range(BLOCKS):
-        inside = (iota((16, 128), 1) + 128 * b).astype(F32) < row_len
-        width = min(128, LONMAX - 128 * b)
-        for out, at in ((out_f, 0), (out_s, 128)):
-            piece = jnp.where(inside, result[16 * b : 16 * b + 16, at : at + 128], 0.0)
-            out[0, :, 128 * b : 128 * b + width] = piece[:, :width]
+        inside = (column + 128 * b).astype(F32) < row_len
+        blocks[16 * b : 16 * b + 16, :] = jnp.where(inside, result[16 * b : 16 * b + 16], 0.0)
 
     @pl.when(own_line)
     def _():
@@ -391,14 +414,21 @@
     pltpu.make_async_copy(gone, gone, ssem2).wait()
 
 
+def lay_out(blocks, out_f, out_s):
+    for b in range(BLOCKS):
+        width = min(128, LONMAX - 128 * b)
+        for out, at in ((out_f, 0), (out_s, 128)):
+            out[0, :, 128 * b : 128 * b + width] = blocks[16 * b : 16 * b + 16, at : at + width]
+
+
 def shards(control, vertical_root, legendre, wave_list, row_length):
     shape = jax.ShapeDtypeStruct((1, 16, LONMAX), F32)
     vmem, hbm = pl.BlockSpec(memory_space=pltpu.VMEM), pl.BlockSpec(memory_space=pl.ANY)
-    return pl.pallas_call(
+    blocks = pl.pallas_call(
         kernel,
-        out_shape=(shape, shape),
+        out_shape=jax.ShapeDtypeStruct((16 * BLOCKS, 256), F32),
         in_specs=[hbm] * 5,
-        out_specs=(vmem, vmem),
+        out_specs=vmem,
         scratch_shapes=[
             pltpu.VMEM((20, 320, 128), BF16),
             pltpu.VMEM((20, 128, 128), BF16),
@@ -418,11 +448,19 @@
             pltpu.VMEM((48, 1280), F32),
             pltpu.VMEM((2560, 256), BF16),
             pltpu.VMEM((656, 2560), BF16),
-            pltpu.SemaphoreType.DMA((5,)),
+            pltpu.VMEM((512, 128), F32),
+            pltpu.VMEM((896, 128), F32),
+            pltpu.VMEM((1280, 128), F32),
+            pltpu.VMEM((640, 128), F32),
+            pltpu.SemaphoreType.DMA((3,)),
+            pltpu.SemaphoreType.DMA((4,)),
+            pltpu.SemaphoreType.DMA((4,)),
+            pltpu.SemaphoreType.DMA,
+            pltpu.SemaphoreType.DMA((8,)),
             pltpu.SemaphoreType.DMA,
             pltpu.SemaphoreType.DMA,
-            pltpu.SemaphoreType.DMA,
-            pltpu.SemaphoreType.DMA,
+            pltpu.SemaphoreType.REGULAR,
+            pltpu.SemaphoreType.REGULAR,
         ],
         compiler_params=pltpu.CompilerParams(
             collective_id=0, has_side_effects=True, vmem_limit_bytes=56 * 2**20
@@ -434,6 +472,9 @@
         wave_list,
         row_length,
     )
+    return pl.pallas_call(
+        lay_out, out_shape=(shape, shape), in_specs=[vmem], out_specs=(vmem, vmem)
+    )(blocks)
 
 
 def solution(mesh):

time: 63.3 us -> 61.3 us (0.968)
  local copies, waits for them, and re-layouts: 3.45 us -> 0 us
  Pallas kernels: 59 us -> 60.4 us
    unnamed x2 -> x0, local copies, waits for them, and re-layouts: 3.45 us -> none
    pallas_call x1 -> x2, Pallas kernels: 59 us -> 60.4 us  [the longest x1 58.5 us: shards(): pl.pallas_call(kernel, out_shape=jax.ShapeDtypeStruct((16 * BLOCKS, 256),...]
where the time goes in v3:
time: 61.3 us; the launch traced here: 61.1 us
  Pallas kernels  60.4 us (99%)
  between operations  0.64 us (1%)
    pallas_call x1, Pallas kernels, shards(): pl.pallas_call(kernel, out_shape=jax.ShapeDtypeStruct((16 * BLOCKS, 256),...  58.5 us
    pallas_call x1, Pallas kernels, shards(): pl.pallas_call(lay_out, out_shape=(shape, shape), in_specs=[vmem], out_sp...  1.97 us

profile of v3, /device:TPU:1, one launch (start us, length us, event | category | flops | bytes accessed | tf_op | source)
XLA Modules:
  0.0 61.1 jit_solution(1000188564844071157)
XLA Ops:
  0.6 58.5 %shard_map.68.blocks = f32[656,256]{1,0:T(8,128)} custom-call(bf16[20,320,128]{2,1,0:T(8,128)(2,1)} %bitcast.2, bf16[20,128,128]{2,1,0:T(8,128)(2,1)} %vert_hbm.1, bf16[640,1280]{1,0:T(8,128)(2,1)} %bitcast.3, s32[1280]{0:T(1024)} %waves_hbm.1, s32[32]{0:T(128)} %rows_hbm.1), custom_call_target="tpu_custom_call" | custom-call | tf_op jit(solution)/shard_map/pallas_call | solution.py:427
  59.1 2.0 %shard_map.69 = (f32[1,16,5136]{2,1,0:T(8,128)}, f32[1,16,5136]{2,1,0:T(8,128)}) custom-call(f32[656,256]{1,0:T(8,128)} %shard_map.68.blocks), custom_call_target="tpu_custom_call" | custom-call | tf_op jit(solution)/shard_map/pallas_call | solution.py:475

commit v4 on v3

--- a/solution.py
+++ b/solution.py
@@ -60,8 +60,8 @@
 def kernel(
     ctrl_hbm, vert_hbm, leg_hbm, waves_hbm, rows_hbm,
     blocks,
-    ctrl, vert, waves, leg, rows_len, prod, send1, recv1, w0, w1, w2, w3, send2, recv2, cos_t, sin_t, basis, tw,
-    acc0, acc1, acc2, acc3,
+    ctrl, vert, waves, leg, rows_len, prod, send1, recv1, w0, w1, w2, w3, staged, send2, recv2, cos_t, sin_t, basis, tw,
+    acc0, acc1, acc2, acc3, total_ref,
     in_sem, ctrl_sem, vert_sem, ssem1, rsem1, ssem2, rsem2, told1, told2,
 ):
     band, lev = lax.axis_index("band"), lax.axis_index("lev")
@@ -259,16 +259,19 @@
     one_lane = iota((1, 128), 1)
 
     def gather_base(o, found):
-        return jnp.where((one_lane & 63) == o, waves[o * 20], found)
-
-    bases = lax.fori_loop(0, 64, gather_base, jnp.zeros((1, 128), jnp.int32))
-    half = lax.shift_right_logical(one_lane, 6)
+        mine = (one_lane & 31) == o
+        return tuple(jnp.where(mine, waves[(32 * h + o) * 20], found[h]) for h in range(2))
+
+    no_base = jnp.zeros((1, 128), jnp.int32)
+    bases = lax.fori_loop(0, 32, gather_base, (no_base, no_base))
+    quarter = lax.shift_right_logical(one_lane, 5)
 
     def tables(tile, carry):
-        fine = lax.rem(tile, 4)
-        pair = lax.div(tile, 4)
-        slots = jnp.where(pair == 2, 16 + 2 * fine + half, 8 * pair + 4 * half + fine)
-        wave = jnp.where(slots < 10, bases + slots, M - 1 - bases - (slots - 10)).astype(F32)
+        part = lax.div(tile, 5)
+        fine = lax.rem(tile, 5)
+        base = jnp.where(part == 0, bases[0], bases[1])
+        slots = jnp.where(fine == 4, 16 + quarter, 4 * quarter + fine)
+        wave = jnp.where(slots < 10, base + slots, M - 1 - base - (slots - 10)).astype(F32)
         cols = pl.ds(pl.multiple_of(tile * 128, 128), 128)
         starts = iota((48, 128), 0).astype(F32) * 128.0
         cosine, sine = turn(starts * wave, row_len, inverse)
@@ -278,8 +281,8 @@
         cosine, sine = turn(columns * wave, row_len, inverse)
         weight = jnp.where(wave == 0.0, 1.0, 2.0)
         slope = weight * wave * (1.0 / M)
-        real = pl.ds(pl.multiple_of(tile * 128, 128), 128)
-        imag = pl.ds(pl.multiple_of(1280 + tile * 128, 128), 128)
+        real = pl.ds(pl.multiple_of((tile + 5 * part) * 128, 128), 128)
+        imag = pl.ds(pl.multiple_of((tile + 5 * part + 5) * 128, 128), 128)
         basis[real, :128] = (cosine * weight).T.astype(BF16)
         basis[imag, :128] = (sine * -weight).T.astype(BF16)
         basis[real, 128:] = (sine * -slope).T.astype(BF16)
@@ -332,74 +335,85 @@
         diagonal(sum4, 64, 128, every),
     )
     for n, group in enumerate(groups):
-        send2.reshape(512, 128)[pl.ds(n, 64, stride=8), :] = group
+        staged.reshape(512, 128)[pl.ds(n, 64, stride=8), :] = group
+    staged.reshape(512, 128)[pl.ds(5, 64, stride=8), :] = jnp.zeros((64, 128), F32)
+    send2[...] = staged[:, :6, :].astype(BF16)
 
     def fourier_row(lat):
         row = jnp.where(lat < 32, lat, 95 - lat)
-        return send2.at[row, pl.ds(0, 5), :], recv2.at[band, pl.ds(0, 5), :]
-
-    def fourier_step(e, carry):
-        lat = lax.rem(z + 4 + 3 * lax.div(e, 8), 8) * 8 + (rc ^ lax.rem(e, 8))
-        src, dst = fourier_row(lat)
-        pltpu.make_async_remote_copy(
-            src_ref=src, dst_ref=dst, send_sem=ssem2, recv_sem=rsem2, device_id=(lat, lev), device_id_type=MESH
-        ).start()
+        return send2.at[row], recv2.at[band]
+
+    def fourier_step(n, carry):
+        plane = lax.rem(z + 4 + 3 * n, 8)
+        for e in range(8):
+            lat = plane * 8 + (rc ^ e)
+            src, dst = fourier_row(lat)
+            copy = pltpu.make_async_remote_copy(
+                src_ref=src, dst_ref=dst, send_sem=ssem2, recv_sem=rsem2.at[half],
+                device_id=(lat, lev), device_id_type=MESH,
+            )
+            if e:
+                copy.start()
+            else:
+                pl.when(n != 4)(copy.start)
         return carry
 
+    half = lax.div(band, 32)
     pl.semaphore_wait(told2, jnp.where(own_line, 7, 8))
     src, dst = fourier_row(band)
-    pltpu.make_async_copy(src, dst, rsem2).start()
-    lax.fori_loop(0, 32, fourier_step, 0)
-    lax.fori_loop(33, 64, fourier_step, 0)
-    arrived = recv2.at[:, pl.ds(0, 5), :]
-    pltpu.make_async_copy(arrived, arrived, rsem2).wait()
-
-    def received(n):
-        return recv2.reshape(512, 128)[pl.ds(n, 64, stride=8), :].astype(BF16).astype(F32)
-
-    first_two = jnp.concatenate([received(0), received(1)], axis=0).T
-    second_two = jnp.concatenate([received(2), received(3)], axis=0).T
-    last_one = received(4)
-    last_one = jnp.concatenate([last_one, last_one], axis=0).T
-    left = iota((16, 128), 1) < 64
-
-    def coefficients(part):
-        tiles = []
-        for source in (first_two, second_two):
-            for fine in range(4):
-                at = fine * 32 + part * 16
-                tiles.append(source[at : at + 16])
-        for fine in (0, 2):
-            at = fine * 32 + part * 16
-            tiles.append(jnp.where(left, last_one[at : at + 16], last_one[at + 32 : at + 48]))
-        return tiles
-
-    reals, imags = coefficients(0), coefficients(1)
-
-    def twist(start, count):
-        for tile in range(10):
-            cols = slice(tile * 128, tile * 128 + 128)
-            imag_cols = slice(1280 + tile * 128, 1408 + tile * 128)
-            cosines, sines = cos_t[pl.ds(start, 8), cols], sin_t[pl.ds(start, 8), cols]
-            real, imag = reals[tile], imags[tile]
-            for n in range(count):
-                at = pl.ds(pl.multiple_of((start + n) * 16, 16), 16)
-                cosine, sine = cosines[n : n + 1], sines[n : n + 1]
-                tw[at, cols] = (real * cosine - imag * sine).astype(BF16)
-                tw[at, imag_cols] = (real * sine + imag * cosine).astype(BF16)
-
-    def twist_step(n, carry):
-        twist(pl.multiple_of(n * 8, 8), 8)
-        return carry
-
-    lax.fori_loop(0, 5, twist_step, 0)
-    twist(40, 1)
-
-    result = dot_nn(tw[...], basis[...])
+    pltpu.make_async_copy(src, dst, rsem2.at[half]).start()
+    lax.fori_loop(0, 8, fourier_step, 0)
+    chunk16 = lax.shift_right_logical(iota((16, 128), 1), 5)
+    for part in range(2):
+        arrived = recv2.at[pl.ds(32 * part, 32)]
+        pltpu.make_async_copy(arrived, arrived, rsem2.at[part]).wait()
+        staged[32 * part : 32 * part + 32, :6, :] = recv2[32 * part : 32 * part + 32].astype(F32)
+
+        def received(n):
+            rows = pl.ds(256 * part + n, 32, stride=8)
+            return staged.reshape(512, 128)[rows, :]
+
+        four = jnp.concatenate([received(n) for n in range(4)], axis=0).T
+        last = jnp.concatenate([received(4)] * 4, axis=0).T
+
+        def coefficients(c):
+            tiles = [four[32 * n + 16 * c : 32 * n + 16 * c + 16] for n in range(4)]
+            mixed = last[16 * c : 16 * c + 16]
+            for n in range(1, 4):
+                mixed = jnp.where(chunk16 == n, last[32 * n + 16 * c : 32 * n + 16 * c + 16], mixed)
+            return tiles + [mixed]
+
+        reals, imags = coefficients(0), coefficients(1)
+
+        def twist(start, count):
+            for tile in range(5):
+                cols = slice((5 * part + tile) * 128, (5 * part + tile) * 128 + 128)
+                real_cols = slice((10 * part + tile) * 128, (10 * part + tile) * 128 + 128)
+                imag_cols = slice((10 * part + tile + 5) * 128, (10 * part + tile + 5) * 128 + 128)
+                cosines, sines = cos_t[pl.ds(start, 8), cols], sin_t[pl.ds(start, 8), cols]
+                real, imag = reals[tile], imags[tile]
+                for n in range(count):
+                    at = pl.ds(pl.multiple_of((start + n) * 16, 16), 16)
+                    cosine, sine = cosines[n : n + 1], sines[n : n + 1]
+                    tw[at, real_cols] = (real * cosine - imag * sine).astype(BF16)
+                    tw[at, imag_cols] = (real * sine + imag * cosine).astype(BF16)
+
+        def twist_step(n, carry):
+            twist(pl.multiple_of(n * 8, 8), 8)
+            return carry
+
+        lax.fori_loop(0, 5, twist_step, 0)
+        twist(40, 1)
+        sums = dot_nn(tw[:, 1280 * part : 1280 * part + 1280], basis[1280 * part : 1280 * part + 1280, :])
+        if part == 0:
+            total_ref[...] = sums
+        else:
+            total = sums
+
     column = iota((16, 256), 1) & 127
     for b in range(BLOCKS):
         inside = (column + 128 * b).astype(F32) < row_len
-        blocks[16 * b : 16 * b + 16, :] = jnp.where(inside, result[16 * b : 16 * b + 16], 0.0)
+        blocks[16 * b : 16 * b + 16, :] = jnp.where(inside, total[16 * b : 16 * b + 16] + total_ref[16 * b : 16 * b + 16, :], 0.0)
 
     @pl.when(own_line)
     def _():
@@ -410,7 +424,7 @@
     def _():
         pltpu.make_async_copy(send1, send1, ssem1).wait()
 
-    gone = send2.at[pl.ds(0, 63), pl.ds(0, 5), :]
+    gone = send2.at[pl.ds(0, 63)]
     pltpu.make_async_copy(gone, gone, ssem2).wait()
 
 
@@ -443,7 +457,8 @@
             pltpu.VMEM((1280, 1024), BF16),
             pltpu.VMEM((640, 1024), BF16),
             pltpu.VMEM((64, 8, 128), F32),
-            pltpu.VMEM((64, 8, 128), F32),
+            pltpu.VMEM((64, 6, 128), BF16),
+            pltpu.VMEM((64, 6, 128), BF16),
             pltpu.VMEM((48, 1280), F32),
             pltpu.VMEM((48, 1280), F32),
             pltpu.VMEM((2560, 256), BF16),
@@ -452,13 +467,14 @@
             pltpu.VMEM((896, 128), F32),
             pltpu.VMEM((1280, 128), F32),
             pltpu.VMEM((640, 128), F32),
+            pltpu.VMEM((656, 256), F32),
             pltpu.SemaphoreType.DMA((3,)),
             pltpu.SemaphoreType.DMA((4,)),
             pltpu.SemaphoreType.DMA((4,)),
             pltpu.SemaphoreType.DMA,
             pltpu.SemaphoreType.DMA((8,)),
             pltpu.SemaphoreType.DMA,
-            pltpu.SemaphoreType.DMA,
+            pltpu.SemaphoreType.DMA((2,)),
             pltpu.SemaphoreType.REGULAR,
             pltpu.SemaphoreType.REGULAR,
         ],

time: 61.3 us -> 59.1 us (0.964)
  Pallas kernels: 60.4 us -> 58.3 us
    pallas_call x1, Pallas kernels: 58.5 us -> 56.3 us  [shards(): pl.pallas_call(kernel, out_shape=jax.ShapeDtypeStruct((16 * BLOCKS, 256),...]
where the time goes in v4:
time: 59.1 us; the launch traced here: 58.9 us
  Pallas kernels  58.3 us (99%)
  between operations  0.64 us (1%)
    pallas_call x1, Pallas kernels, shards(): pl.pallas_call(kernel, out_shape=jax.ShapeDtypeStruct((16 * BLOCKS, 256),...  56.3 us
    pallas_call x1, Pallas kernels, shards(): pl.pallas_call(lay_out, out_shape=(shape, shape), in_specs=[vmem], out_sp...  1.97 us

profile of v4, /device:TPU:1, one launch (start us, length us, event | category | flops | bytes accessed | tf_op | source)
XLA Modules:
  0.0 58.9 jit_solution(4561747229379184949)
XLA Ops:
  0.6 56.3 %shard_map.68.blocks = f32[656,256]{1,0:T(8,128)} custom-call(bf16[20,320,128]{2,1,0:T(8,128)(2,1)} %bitcast.2, bf16[20,128,128]{2,1,0:T(8,128)(2,1)} %vert_hbm.1, bf16[640,1280]{1,0:T(8,128)(2,1)} %bitcast.3, s32[1280]{0:T(1024)} %waves_hbm.1, s32[32]{0:T(128)} %rows_hbm.1), custom_call_target="tpu_custom_call" | custom-call | tf_op jit(solution)/shard_map/pallas_call | solution.py:441
  57.0 2.0 %shard_map.69 = (f32[1,16,5136]{2,1,0:T(8,128)}, f32[1,16,5136]{2,1,0:T(8,128)}) custom-call(f32[656,256]{1,0:T(8,128)} %shard_map.68.blocks), custom_call_target="tpu_custom_call" | custom-call | tf_op jit(solution)/shard_map/pallas_call | solution.py:491

commit v5 on v4

--- a/solution.py
+++ b/solution.py
@@ -80,22 +80,22 @@
         pltpu.make_async_copy(src, dst, in_sem.at[n])
         for n, (src, dst) in enumerate(((waves_hbm, waves), (leg_hbm, leg), (rows_hbm, rows_len)))
     ]
+    barrier = pltpu.get_barrier_semaphore()
+
+    def greet(e, carry):
+        @pl.when(jnp.logical_not(jnp.logical_and(e == band, own_line)))
+        def _():
+            pl.semaphore_signal(barrier, inc=1, device_id=(e, z), device_id_type=MESH)
+
+        return carry
+
+    lax.fori_loop(0, 64, greet, 0)
     for q in range(4):
         for copy in chunk_copies(q):
             copy.start()
     for copy in copies:
         copy.start()
 
-    barrier = pltpu.get_barrier_semaphore()
-
-    def greet(e, carry):
-        @pl.when(jnp.logical_not(jnp.logical_and(e == band, own_line)))
-        def _():
-            pl.semaphore_signal(barrier, inc=1, device_id=(e, z), device_id_type=MESH)
-
-        return carry
-
-    lax.fori_loop(0, 64, greet, 0)
     def products(q, carry):
         for copy in chunk_copies(q):
             copy.wait()
@@ -167,7 +167,7 @@
                 send1[8 * d + y, 16 * tile : 16 * tile + 16, :] = jnp.concatenate([top[y], low[y]], axis=0).astype(BF16)
         low = exchange([extra_b(r) for r in range(8)])
         for y in range(8):
-            send1[8 * d + y, 48:56, :] = low[y].astype(BF16)
+            send1[8 * d + y, 48:54, :] = low[y][:6].astype(BF16)
 
         for e in (4, 3, 5, 2, 6, 1, 7, 0):
             y = lax.rem(lev + e, 8)
@@ -298,8 +298,8 @@
         count = 16 * (last - first)
         if n < 3:
             return recv1[first:last, 16 * n : 16 * n + 16, :].reshape(count, 128)
-        rest = recv1[first:last, 48:56, :]
-        return jnp.concatenate([rest, jnp.zeros_like(rest)], axis=1).reshape(count, 128)
+        rest = recv1[first:last, 48:54, :]
+        return jnp.concatenate([rest, jnp.zeros((last - first, 10, 128), BF16)], axis=1).reshape(count, 128)
 
     def diagonal(value, start, step, where_chunks):
         total = None
@@ -450,8 +450,8 @@
             pltpu.VMEM((640, 1280), BF16),
             pltpu.SMEM((32,), jnp.int32),
             pltpu.VMEM((32 * 320, 128), F32),
-            pltpu.VMEM((64, 56, 128), BF16),
-            pltpu.VMEM((64, 56, 128), BF16),
+            pltpu.VMEM((64, 54, 128), BF16),
+            pltpu.VMEM((64, 54, 128), BF16),
             pltpu.VMEM((512, 1024), BF16),
             pltpu.VMEM((896, 1024), BF16),
             pltpu.VMEM((1280, 1024), BF16),

time: 59.1 us -> 59.1 us (level)
  no operation moved by 1% of the time
where the time goes in v5:
time: 59.1 us; the launch traced here: 58.9 us
  Pallas kernels  58.3 us (99%)
  between operations  0.64 us (1%)
    pallas_call x1, Pallas kernels, shards(): pl.pallas_call(kernel, out_shape=jax.ShapeDtypeStruct((16 * BLOCKS, 256),...  56.3 us
    pallas_call x1, Pallas kernels, shards(): pl.pallas_call(lay_out, out_shape=(shape, shape), in_specs=[vmem], out_sp...  1.97 us

profile of v5, /device:TPU:1, one launch (start us, length us, event | category | flops | bytes accessed | tf_op | source)
XLA Modules:
  0.0 58.9 jit_solution(2862680721870079531)
XLA Ops:
  0.6 56.3 %shard_map.68.blocks = f32[656,256]{1,0:T(8,128)} custom-call(bf16[20,320,128]{2,1,0:T(8,128)(2,1)} %bitcast.2, bf16[20,128,128]{2,1,0:T(8,128)(2,1)} %vert_hbm.1, bf16[640,1280]{1,0:T(8,128)(2,1)} %bitcast.3, s32[1280]{0:T(1024)} %waves_hbm.1, s32[32]{0:T(128)} %rows_hbm.1), custom_call_target="tpu_custom_call" | custom-call | tf_op jit(solution)/shard_map/pallas_call | solution.py:441
  56.9 2.0 %shard_map.69 = (f32[1,16,5136]{2,1,0:T(8,128)}, f32[1,16,5136]{2,1,0:T(8,128)}) custom-call(f32[656,256]{1,0:T(8,128)} %shard_map.68.blocks), custom_call_target="tpu_custom_call" | custom-call | tf_op jit(solution)/shard_map/pallas_call | solution.py:491
